TPU v7x, 32 devices: a whole 2x2x4 slice. The times are simulated.
32 devices in a mesh: row: 4 (over y, x), col: 8 (over z, core).
Axes of the slice: x: 2, y: 2, z: 4, core: 2. Of those that a mesh axis runs over, the one named last changes fastest.
Arguments:
- corner: float32 [18432, 18432], P('row', 'col'), may hold values from -0.046875 to 0.046875
- right_proj: float32 [18432, 512], P('col', 'row'), may hold values from -1.5 to 1.5
- left_proj: float32 [18432, 512], P('row', 'col'), may hold values from -1.5 to 1.5
- upstream: float32 [512, 512], replicated, may hold values from -0.25 to 0.25
Outputs:
- corner_right: float32 [18432, 512], P(('row', 'col'))
- corner_left: float32 [18432, 512], P(('col', 'row'))
- right_grad: float32 [18432, 512], P(('col', 'row'))
- left_grad: float32 [18432, 512], P(('row', 'col'))
- corner_grad: float32 [18432, 18432], P('row', 'col')
All inputs are finite; a program needn't handle non-finite values.
Results may differ from a plain program's by a relative error of at most 0.00007.
Values sent between devices are 32-bit elements; how exact they have to be, the bound alone decides.
A program may use at most 192 MiB of HBM per device.

v0:
```python
import jax
import jax.numpy as jnp
from jax import lax
from jax.sharding import PartitionSpec as P


def body(corner, right_proj, left_proj, upstream):
    best = lax.Precision.HIGHEST
    piece = lax.all_gather(left_proj, "col", axis=1, tiled=True)
    block = lax.dot_general(
        corner, piece, (((0,), (0,)), ((), ())), precision=best, preferred_element_type=jnp.float32
    )
    partial_left = block
    fold_weighted = jnp.dot(piece, upstream, precision=best, preferred_element_type=jnp.float32)
    partial_left, weighted = (partial_left, fold_weighted)
    piece = lax.all_gather(right_proj, "row", axis=1, tiled=True)
    block = jnp.dot(corner, piece, precision=best, preferred_element_type=jnp.float32)
    partial_right = block
    grad_tile = lax.dot_general(
        weighted,
        piece,
        (((1,), (1,)), ((), ())),
        precision=best,
        preferred_element_type=jnp.float32,
    )
    partial_right, corner_grad = (partial_right, grad_tile)
    corner_right = lax.psum_scatter(partial_right, "col", scatter_dimension=0, tiled=True)
    corner_left = lax.psum_scatter(partial_left, "row", scatter_dimension=0, tiled=True)
    right_grad = jnp.dot(corner_left, upstream, precision=best, preferred_element_type=jnp.float32)
    left_grad = lax.dot_general(
        corner_right,
        upstream,
        (((1,), (1,)), ((), ())),
        precision=best,
        preferred_element_type=jnp.float32,
    )
    return (corner_right, corner_left, right_grad, left_grad, corner_grad)


def solution(mesh):
    placed = (P("row", "col"), P("col", "row"), P("row", "col"), P())
    return jax.shard_map(
        body,
        mesh=mesh,
        in_specs=placed,
        out_specs=(
            P(("row", "col"), None),
            P(("col", "row"), None),
            P(("col", "row"), None),
            P(("row", "col"), None),
            P("row", "col"),
        ),
        check_vma=False,
    )
```

profile of v0, /device:TPU:0, one launch (start us, length us, event | category | flops | bytes accessed | tf_op | source)
XLA Modules:
  0.0 434.4 jit_solution(6080459211284178451)
XLA Ops:
  7.2 0.0 copy-start
  7.2 0.0 all-gather.5.cloned.1.call-start
  7.2 0.7 all-gather.5.cloned.1.call-update
  7.9 0.0 all-gather.3.cloned.1.call-start
  8.0 0.7 all-gather.3.cloned.1.call-update
  8.7 0.0 reduce-scatter.5.cloned.1.call-start
  8.7 94.4 %all-gather.5.cloned.1.call-done = f32[4608,512]{0,1:T(8,128)} async-done(((f32[4608,64]{0,1:T(8,128)}), f32[4608,512]{0,1:T(8,128)}) %all-gather.5.cloned.1.call-update) | async-done | bytes 9437200 | tf_op jit(solution)/shard_map/all_gather | solution.py:9
  103.1 138.3 %fusion.1 = f32[2304,512]{1,0:T(8,128)} fusion(f32[4608,2304]{1,0:T(8,128)} %param.4, f32[4608,512]{0,1:T(8,128)} %all-gather.5.cloned.1.call-done), kind=kOutput, calls=%fused_computation.1 | convolution fusion | flops 65229815808 | bytes 56623104 | tf_op jit(solution)/shard_map/dot_general | solution.py:10
  241.4 0.0 reduce-scatter.5.cloned.1.call-update
  241.4 0.0 reduce-scatter.3.cloned.1.call-start
  241.5 0.0 all-gather.3.cloned.1.call-done
  241.5 83.5 %fusion = f32[4608,512]{1,0:T(8,128)} fusion(f32[4608,2304]{1,0:T(8,128)} %param.4, f32[2304,512]{1,0:T(8,128)} %all-gather.3.cloned.1.call-done), kind=kOutput, calls=%fused_computation | convolution fusion | flops 65229815808 | bytes 56623104 | tf_op jit(solution)/shard_map/dot_general | solution.py:17
  325.0 0.0 slice-start
  325.1 0.0 reduce-scatter.3.cloned.1.call-update
  325.1 0.0 copy-done
  325.1 0.0 slice-start.1
  325.1 18.6 %fusion.4 = f32[4608,512]{1,0:T(8,128)S(1)} fusion(f32[4608,512]{0,1:T(8,128)} %all-gather.5.cloned.1.call-done, f32[512,512]{1,0:T(8,128)S(1)} %copy-done), kind=kOutput, calls=%fused_computation.4 | convolution fusion | flops 14495514624 | bytes 19922944 | tf_op jit(solution)/shard_map/dot_general | solution.py:14
  343.7 0.0 slice-done
  343.8 0.0 slice-done.1
  343.8 72.1 %fusion.5 = f32[4608,2304]{1,0:T(8,128)} fusion(f32[4608,512]{1,0:T(8,128)S(1)} %fusion.4, f32[2304,512]{1,0:T(8,128)S(1)} %bitcast.13), kind=kOutput, calls=%fused_computation.5 | convolution fusion | flops 65229815808 | bytes 56623104 | tf_op jit(solution)/shard_map/dot_general | solution.py:19
  415.9 0.0 reduce-scatter.5.cloned.1.call-done
  415.9 4.4 %fusion.2 = f32[576,512]{1,0:T(8,128)} fusion(f32[576,512]{1,0:T(8,128)} %reduce-scatter.5.cloned.1.call-done, f32[512,512]{1,0:T(8,128)S(1)} %copy-done), kind=kOutput, calls=%fused_computation.2 | convolution fusion | flops 1811939328 | bytes 3407872 | tf_op jit(solution)/shard_map/dot_general | solution.py:29
  420.3 2.9 reduce-scatter.3.cloned.1.call-done
  423.2 4.3 %fusion.3 = f32[576,512]{1,0:T(8,128)} fusion(f32[576,512]{1,0:T(8,128)} %reduce-scatter.3.cloned.1.call-done, f32[512,512]{1,0:T(8,128)S(1)} %copy-done), kind=kOutput, calls=%fused_computation.3 | convolution fusion | flops 1811939328 | bytes 3407872 | tf_op jit(solution)/shard_map/dot_general | solution.py:30
  (1 shorter events, 0.0 us)
Async XLA Ops:
  7.2 317.9 %copy-start = (f32[512,512]{1,0:T(8,128)S(1)}, f32[512,512]{1,0:T(8,128)}, u32[]{:S(2)}) copy-start(f32[512,512]{1,0:T(8,128)} %param.7) | copy-start | bytes 3145732
  7.2 95.9 %all-gather.5.cloned.1.call-start = ((), (), s32[]{:S(2)}) async-start(), calls=%async_computation.4 | async-start | bytes 10616832 | tf_op jit(solution)/shard_map/all_gather | solution.py:9
  7.9 233.6 %all-gather.3.cloned.1.call-start = ((), (), s32[]{:S(2)}) async-start(), calls=%async_computation.2 | async-start | bytes 5898240 | tf_op jit(solution)/shard_map/all_gather | solution.py:16
  8.7 407.2 %reduce-scatter.5.cloned.1.call-start = ((), (), s32[]{:S(2)}) async-start(), calls=%async_computation.5 | async-start | bytes 5898240 | tf_op jit(solution)/shard_map/reduce_scatter | solution.py:28
  241.4 181.8 %reduce-scatter.3.cloned.1.call-start = ((), (), s32[]{:S(2)}) async-start(), calls=%async_computation.3 | async-start | bytes 10616832 | tf_op jit(solution)/shard_map/reduce_scatter | solution.py:27
  325.0 18.7 %slice-start = ((s8[4718592]{0:T(1024)(128)(4,1)}), s8[524288]{0:T(1024)(128)(4,1)S(1)}, s32[]{:S(2)}) async-start(s8[4718592]{0:T(1024)(128)(4,1)} %bitcast.12), calls=%async_computation.6 | async-start | bytes 1048576
  325.1 18.7 %slice-start.1 = ((s8[4718592]{0:T(1024)(128)(4,1)}), s8[4194304]{0:T(1024)(128)(4,1)S(1)}, s32[]{:S(2)}) async-start(s8[4718592]{0:T(1024)(128)(4,1)} %bitcast.12), calls=%async_computation.7 | async-start | bytes 8388608
Sparse Core Ops, SparseCore 0:
  9.7 93.4 all-gather.4
  104.9 55.3 all-gather.2
  241.6 55.5 reduce-scatter.4
  325.2 97.9 reduce-scatter.2
where the time goes:
time: 435 us; the launch traced here: 434 us
  matrix products  321 us (74%)
  waiting for transfers between devices  98.8 us (23%)
  between operations  14.1 us (3%)
    dot_general x1, matrix products, body(): lax.dot_general(corner, piece, (((0,), (0,)), ((), ())), precision=best,...  138 us
    all_gather x1, waiting for transfers between devices, body(): piece = lax.all_gather(left_proj, 'col', axis=1, tiled=True)  94.4 us
    dot_general x1, matrix products, body(): jnp.dot(corner, piece, precision=best, preferred_element_type=jnp.float32)  83.5 us
    dot_general x1, matrix products, body(): lax.dot_general(weighted, piece, (((1,), (1,)), ((), ())), precision=best...  72.1 us
    dot_general x1, matrix products, body(): jnp.dot(piece, upstream, precision=best, preferred_element_type=jnp.float32)  18.6 us
  transfers between devices with their start and end apart: 4, of which 2 were waited for; matrix products, arithmetic and copies ran while one was open for 73% of the time, Pallas kernels for 0%

commit v1 on v0

v1 whole, which is shorter than its diff:
```python
import functools

import jax
import jax.numpy as jnp
from jax import lax
from jax.experimental import pallas as pl
from jax.experimental.pallas import tpu as pltpu
from jax.sharding import PartitionSpec as P

VMEM = 60 * 1024 * 1024


def split(x):
    high = x.astype(jnp.bfloat16)
    return high, (x - high.astype(jnp.float32)).astype(jnp.bfloat16)


def product(a, b):
    dot = functools.partial(jnp.dot, preferred_element_type=jnp.float32)
    return dot(a[0], b[0]) + (dot(a[0], b[1]) + dot(a[1], b[0]))


def block_of(size, limit, unit):
    fits = [n for n in range(unit, limit + 1, unit) if size % n == 0]
    return fits[-1] if fits else size


def call(kernel, grid, ins, out_spec, out_shape, scratch, flops, moved):
    return pl.pallas_call(
        kernel,
        grid=grid,
        in_specs=ins,
        out_specs=out_spec,
        out_shape=jax.ShapeDtypeStruct(out_shape, jnp.float32),
        scratch_shapes=scratch,
        compiler_params=pltpu.CompilerParams(vmem_limit_bytes=VMEM),
        cost_estimate=pl.CostEstimate(flops=flops, bytes_accessed=moved, transcendentals=0),
    )


def whole(shape):
    return pl.BlockSpec(shape, lambda i: (0, 0), pipeline_mode=pl.Buffered(1))


def right_kernel(corner_ref, proj_ref, out_ref, high, low):
    @pl.when(pl.program_id(0) == 0)
    def _():
        high[...], low[...] = split(proj_ref[...])

    out_ref[...] = product(split(corner_ref[...]), (high[...], low[...]))


def right_product(corner, proj, parts, chunk, chunks):
    rows, depth = corner.shape
    chi = proj.shape[1]
    tile = rows // parts // chunks
    return call(
        right_kernel,
        (parts,),
        [pl.BlockSpec((tile, depth), lambda i: (i * chunks + chunk, 0)), whole((depth, chi))],
        pl.BlockSpec((tile, chi), lambda i: (i, 0)),
        (rows // chunks, chi),
        [pltpu.VMEM((depth, chi), jnp.bfloat16)] * 2,
        6 * rows * depth * chi // chunks,
        4 * rows * depth // chunks,
    )(corner, proj)


def left_kernel(corner_ref, proj_ref, out_ref, high, low):
    @pl.when(pl.program_id(0) == 0)
    def _():
        high[...], low[...] = split(proj_ref[...])

    out_ref[...] = product((high[...], low[...]), split(corner_ref[...])).T


def left_product(corner, proj_t):
    rows, width = corner.shape
    chi = proj_t.shape[0]
    tile = block_of(width, 256, 128)
    return call(
        left_kernel,
        (width // tile,),
        [pl.BlockSpec((rows, tile), lambda i: (0, i)), whole((chi, rows))],
        pl.BlockSpec((tile, chi), lambda i: (i, 0)),
        (width, chi),
        [pltpu.VMEM((chi, rows), jnp.bfloat16)] * 2,
        6 * rows * width * chi,
        4 * rows * width,
    )(corner, proj_t)


def grad_kernel(left_ref, up_ref, right_ref, out_ref, high, low):
    @pl.when(pl.program_id(0) == 0)
    def _():
        high[...], low[...] = split(product(split(up_ref[...]), split(right_ref[...].T)))

    out_ref[...] = product(split(left_ref[...].T), (high[...], low[...]))


def grad_product(proj_t, upstream, right):
    chi, rows = proj_t.shape
    width = right.shape[0]
    tile = block_of(rows, 512, 128)
    return call(
        grad_kernel,
        (rows // tile,),
        [pl.BlockSpec((chi, tile), lambda i: (0, i)), whole((chi, chi)), whole((width, chi))],
        pl.BlockSpec((tile, width), lambda i: (i, 0)),
        (rows, width),
        [pltpu.VMEM((chi, width), jnp.bfloat16)] * 2,
        6 * rows * width * chi,
        4 * rows * width,
    )(proj_t, upstream, right)


def swaps(name, n):
    me = lax.axis_index(name)
    for step in range(1, n):
        if n & (n - 1):
            yield [(i, (i + step) % n) for i in range(n)], (me + step) % n, (me - step + n) % n
        else:
            yield [(i, i ^ step) for i in range(n)], me ^ step, me ^ step


def gather(x, name, n, axis):
    size = x.shape[axis]
    shape = list(x.shape)
    shape[axis] = n * size
    got = [(lax.axis_index(name), x)]
    got += [(source, lax.ppermute(x, name, pairs)) for pairs, _, source in swaps(name, n)]
    out = jnp.zeros(shape, x.dtype)
    for owner, block in got:
        out = lax.dynamic_update_slice_in_dim(out, block, owner * size, axis)
    return out


def scatter_sum(x, name, n):
    size = x.shape[0] // n
    mine = functools.partial(lax.dynamic_slice_in_dim, x, slice_size=size, axis=0)
    total = mine(lax.axis_index(name) * size)
    for pairs, target, _ in swaps(name, n):
        total += lax.ppermute(mine(target * size), name, pairs)
    return total


def body(rows, parts, corner, right_proj, left_proj, upstream):
    high = lax.Precision.HIGH
    chunks = 1
    right = gather(right_proj, "row", rows, 1)
    left_t = lax.all_gather(left_proj.T, "col", axis=0, tiled=True)
    pieces = [right_product(corner, right, parts, c, chunks) for c in range(chunks)]
    pieces, left_t = lax.optimization_barrier((pieces, left_t))
    pieces = [lax.psum_scatter(p, "col", scatter_dimension=0, tiled=True) for p in pieces]
    partial_left = left_product(corner, left_t)
    corner_left = scatter_sum(partial_left, "row", rows)
    corner_grad = grad_product(left_t, upstream, right)
    corner_right = jnp.concatenate(pieces, axis=0)
    right_grad = jnp.dot(corner_left, upstream, precision=high, preferred_element_type=jnp.float32)
    left_grad = lax.dot_general(
        corner_right, upstream, (((1,), (1,)), ((), ())), precision=high, preferred_element_type=jnp.float32
    )
    return (corner_right, corner_left, right_grad, left_grad, corner_grad)


def solution(mesh):
    return jax.shard_map(
        functools.partial(body, mesh.shape["row"], mesh.shape["col"]),
        mesh=mesh,
        in_specs=(P("row", "col"), P("col", "row"), P("row", "col"), P()),
        out_specs=(
            P(("row", "col"), None),
            P(("col", "row"), None),
            P(("col", "row"), None),
            P(("row", "col"), None),
            P("row", "col"),
        ),
        check_vma=False,
    )
```

time: 435 us -> 221 us (0.51)
  matrix products: 321 us -> 5.54 us
  Pallas kernels: 0 us -> 129 us
  waiting for transfers between devices: 98.8 us -> 47.3 us
  local copies, waits for them, and re-layouts: 0.02 us -> 14.3 us
  starting transfers between devices: 0.16 us -> 8.02 us
    dot_general x5 -> x1, matrix products: 317 us -> 2.13 us  [body(): jnp.dot(corner_left, upstream, precision=high, preferred_element_type=jnp...]
    pallas_call x0 -> x3, Pallas kernels: none -> 129 us  [the longest x1 46.3 us: grad_product(): call(grad_kernel, (rows // tile,), [pl.BlockSpec((chi, tile), lambda i: (...]
    all_gather x2 -> x1, waiting for transfers between devices: 94.4 us -> 0.01 us  [body(): left_t = lax.all_gather(left_proj.T, 'col', axis=0, tiled=True)]
    ppermute x0 -> x6, waiting for transfers between devices: none -> 46.6 us  [the longest x3 44.7 us: gather(): lax.ppermute(x, name, pairs)]
    ppermute x0 -> x6, starting transfers between devices: none -> 7.95 us  [the longest x3 4.46 us: gather(): lax.ppermute(x, name, pairs)]
    dynamic_update_slice x0 -> x4, local copies, waits for them, and re-layouts: none -> 6.04 us  [gather(): out = lax.dynamic_update_slice_in_dim(out, block, owner * size, axis)]
  transfers between devices with their start and end apart: 4 -> 8, of which waited for: 2 -> 4; matrix products, arithmetic and copies ran while one was open for 73% -> 8% of each run, Pallas kernels for 0% -> 58%
where the time goes in v1:
time: 221 us
  Pallas kernels  129 us (58%)
  waiting for transfers between devices  47.3 us (21%)
  local copies, waits for them, and re-layouts  14.3 us (6%)
  between operations  14.1 us (6%)
  starting transfers between devices  8.02 us (4%)
  matrix products  5.54 us (3%)
  other arithmetic  2.6 us (1%)
    pallas_call x1, Pallas kernels, grad_product(): call(grad_kernel, (rows // tile,), [pl.BlockSpec((chi, tile), lambda i: (...  46.3 us
    ppermute x3, waiting for transfers between devices, gather(): lax.ppermute(x, name, pairs)  44.7 us
    pallas_call x1, Pallas kernels, left_product(): call(left_kernel, (width // tile,), [pl.BlockSpec((rows, tile), lambda i:...  42.7 us
    pallas_call x1, Pallas kernels, right_product(): call(right_kernel, (parts,), [pl.BlockSpec((tile, depth), lambda i: (i *...  40 us
    dynamic_update_slice x4, local copies, waits for them, and re-layouts, gather(): out = lax.dynamic_update_slice_in_dim(out, block, owner * size, axis)  6.04 us
    ppermute x3, starting transfers between devices, gather(): lax.ppermute(x, name, pairs)  4.46 us
  transfers between devices with their start and end apart: 8, of which 4 were waited for; matrix products, arithmetic and copies ran while one was open for 8% of the time, Pallas kernels for 58%

profile of v1, /device:TPU:0, one launch (start us, length us, event | category | flops | bytes accessed | tf_op | source)
XLA Modules:
  0.0 220.9 jit_solution(3255658733774623598)
XLA Ops:
  7.2 0.0 copy-start.2
  7.2 0.0 all-gather.2.cloned.1.call-start
  7.2 0.7 all-gather.2.cloned.1.call-update
  7.9 0.0 reduce-scatter.2.cloned.1.call-start
  8.0 0.5 copy-done.2
  8.4 2.9 %collective-permute-start = (f32[2304,128]{1,0:T(8,128)S(1)}, f32[2304,128]{1,0:T(8,128)}, u32[]{:S(2)}, u32[]{:S(2)}) collective-permute-start(f32[2304,128]{1,0:T(8,128)S(1)} %copy-done.2), channel_id=1, source_target_pairs={{0,8},{8,0},{16,24},{24,16},{1,9},{9,1},{17,25},{25,17},{2,10},{10... | collective-permute-start | bytes 3538952 | tf_op jit(solution)/shard_map/ppermute | solution.py:131
  11.4 1.5 collective-permute-start.1
  12.9 0.0 collective-permute-start.2
  12.9 2.8 %broadcast_in_dim.3 = f32[2304,512]{1,0:T(8,128)} broadcast(f32[]{:T(128)} %constant.10.clone.1), dimensions={} | broadcast | bytes 4718596 | tf_op jit(solution)/shard_map/broadcast_in_dim | solution.py:132
  15.7 1.2 constant_dynamic-update-slice_fusion.3
  16.9 21.3 %collective-permute-done = f32[2304,128]{1,0:T(8,128)} collective-permute-done((f32[2304,128]{1,0:T(8,128)S(1)}, f32[2304,128]{1,0:T(8,128)}, u32[]{:S(2)}, u32[]{:S(2)}) %collective-permute-start) | collective-permute-done | bytes 1179680 | tf_op jit(solution)/shard_map/ppermute | solution.py:131
  38.3 2.5 %constant_dynamic-update-slice_fusion.2 = f32[2304,512]{1,0:T(8,128)} fusion(f32[2304,512]{1,0:T(8,128)} %constant_dynamic-update-slice_fusion.3, f32[2304,128]{1,0:T(8,128)} %collective-permute-done, s32[]{:T(128)S(6)} %select_n.25), kind=kLoop, calls=%fused_computation.6 | loop fusion | bytes 2359300 | tf_op jit(solution)/shard_map/dynamic_update_slice | solution.py:134
  40.7 23.3 %collective-permute-done.1 = f32[2304,128]{1,0:T(8,128)S(1)} collective-permute-done((f32[2304,128]{1,0:T(8,128)S(1)}, f32[2304,128]{1,0:T(8,128)S(1)}, u32[]{:S(2)}, u32[]{:S(2)}) %collective-permute-start.1) | collective-permute-done | bytes 1179680 | tf_op jit(solution)/shard_map/ppermute | solution.py:131
  64.1 1.2 constant_dynamic-update-slice_fusion.1
  65.3 0.0 collective-permute-done.2
  65.3 1.1 constant_dynamic-update-slice_fusion.proj_ref.right_ref
  66.4 40.0 %shard_map.83 = f32[4608,512]{1,0:T(8,128)} custom-call(f32[4608,2304]{1,0:T(8,128)} %corner_ref.3, f32[2304,512]{1,0:T(8,128)} %constant_dynamic-update-slice_fusion.proj_ref.right_ref), custom_call_target="tpu_custom_call" | custom-call | flops 32614907904 | bytes 42467328 | tf_op jit(solution)/shard_map/pallas_call | solution.py:57
  106.5 0.0 all-gather.2.cloned.1.call-done.proj_ref.left_ref
  106.5 0.0 reduce-scatter.2.cloned.1.call-update
  106.5 42.7 %shard_map.84 = f32[2304,512]{1,0:T(8,128)} custom-call(f32[4608,2304]{1,0:T(8,128)} %corner_ref.3, f32[512,4608]{1,0:T(8,128)} %all-gather.2.cloned.1.call-done.proj_ref.left_ref), custom_call_target="tpu_custom_call" | custom-call | flops 32614907904 | bytes 42467328 | tf_op jit(solution)/shard_map/pallas_call | solution.py:81
  149.2 3.9 %constant_dynamic-slice_fusion.2 = (f32[576,512]{1,0:T(8,128)}, f32[576,512]{1,0:T(8,128)}, f32[576,512]{1,0:T(8,128)}) fusion(f32[2304,512]{1,0:T(8,128)} %shard_map.84, s32[]{:T(128)S(6)} %select_n.29, s32[]{:T(128)S(6)} %select_n.31, s32[]{:T(128)S(6)} %select_n.30), kind=kLoop, calls=%fused_computation.3 | loop fusion | bytes 7077900 | tf_op jit(solution)/shard_map/dynamic_slice | solution.py:143
  153.1 0.1 collective-permute-start.3
  153.3 2.9 %collective-permute-start.5 = (f32[576,512]{1,0:T(8,128)}, f32[576,512]{1,0:T(8,128)S(1)}, u32[]{:S(2)}, u32[]{:S(2)}) collective-permute-start(f32[576,512]{1,0:T(8,128)} %get-tuple-element.10), channel_id=1, source_target_pairs={{0,24},{8,16},{16,8},{24,0},{1,25},{9,17},{17,9},{25,1},{2,26},{10... | collective-permute-start | bytes 3538952 | tf_op jit(solution)/shard_map/ppermute | solution.py:143
  156.2 0.5 collective-permute-start.4
  156.6 46.3 %shard_map.85 = f32[4608,2304]{1,0:T(8,128)} custom-call(f32[512,4608]{1,0:T(8,128)} %all-gather.2.cloned.1.call-done.proj_ref.left_ref, f32[512,512]{1,0:T(8,128)} %up_ref.1, f32[2304,512]{1,0:T(8,128)} %constant_dynamic-update-slice_fusion.proj_ref.right_ref), custom_call_target="tpu_custom_call" | custom-call | flops 32614907904 | bytes 42467328 | tf_op jit(solution)/shard_map/pallas_call | solution.py:105
  202.9 0.0 copy-start.1
  202.9 0.0 collective-permute-done.3
  202.9 1.5 collective-permute-done.5
  204.4 0.0 copy-start.3
  204.4 1.0 copy-done.3
  205.4 0.5 collective-permute-done.4
  205.9 2.6 %add_add_fusion = f32[576,512]{1,0:T(8,128)S(1)} fusion(f32[576,512]{1,0:T(8,128)} %copy-done.3, f32[576,512]{1,0:T(8,128)} %collective-permute-done.4, f32[576,512]{1,0:T(8,128)S(1)} %collective-permute-done.3, f32[2304,512]{1,0:T(8,128)} %shard_map.84, s32[]{:T(128)S(6)} %select_n.28), kind=kLoop, calls=%fused_computation | loop fusion | flops 884736 | bytes 5898244 | tf_op jit(solution)/shard_map/add | solution.py:143
  208.5 0.0 copy-done.1
  208.5 0.0 copy-start
  208.5 2.1 fusion
  210.6 0.0 copy-done
  210.6 0.0 reduce-scatter.2.cloned.1.call-done
  210.6 3.4 %fusion.1 = f32[576,512]{1,0:T(8,128)} fusion(f32[576,512]{1,0:T(8,128)} %reduce-scatter.2.cloned.1.call-done, f32[512,512]{1,0:T(8,128)S(1)} %copy-done.1), kind=kOutput, calls=%fused_computation.9 | convolution fusion | flops 905969664 | bytes 3407872 | tf_op jit(solution)/shard_map/dot_general | solution.py:160
Async XLA Ops:
  7.2 1.3 copy-start.2
  7.2 99.3 %all-gather.2.cloned.1.call-start = ((), (), s32[]{:S(2)}) async-start(), calls=%async_computation.1 | async-start | bytes 10616832 | tf_op jit(solution)/shard_map/all_gather | solution.py:151
  7.9 202.7 %reduce-scatter.2.cloned.1.call-start = ((), (), s32[]{:S(2)}) async-start(), calls=%async_computation.2 | async-start | bytes 10616832 | tf_op jit(solution)/shard_map/reduce_scatter | solution.py:154
  8.4 29.8 %collective-permute-start = (f32[2304,128]{1,0:T(8,128)S(1)}, f32[2304,128]{1,0:T(8,128)}, u32[]{:S(2)}, u32[]{:S(2)}) collective-permute-start(f32[2304,128]{1,0:T(8,128)S(1)} %copy-done.2), channel_id=1, source_target_pairs={{0,8},{8,0},{16,24},{24,16},{1,9},{9,1},{17,25},{25,17},{2,10},{10... | collective-permute-start | bytes 3538952 | tf_op jit(solution)/shard_map/ppermute | solution.py:131
  11.4 52.7 %collective-permute-start.1 = (f32[2304,128]{1,0:T(8,128)S(1)}, f32[2304,128]{1,0:T(8,128)S(1)}, u32[]{:S(2)}, u32[]{:S(2)}) collective-permute-start(f32[2304,128]{1,0:T(8,128)S(1)} %copy-done.2), channel_id=1, source_target_pairs={{0,16},{8,24},{16,0},{24,8},{1,17},{9,25},{17,1},{25,9},{2,18},{10... | collective-permute-start | bytes 3538952 | tf_op jit(solution)/shard_map/ppermute | solution.py:131
  12.9 52.4 %collective-permute-start.2 = (f32[2304,128]{1,0:T(8,128)S(1)}, f32[2304,128]{1,0:T(8,128)S(1)}, u32[]{:S(2)}, u32[]{:S(2)}) collective-permute-start(f32[2304,128]{1,0:T(8,128)S(1)} %copy-done.2), channel_id=1, source_target_pairs={{0,24},{8,16},{16,8},{24,0},{1,25},{9,17},{17,9},{25,1},{2,26},{10... | collective-permute-start | bytes 3538952 | tf_op jit(solution)/shard_map/ppermute | solution.py:131
  153.1 49.8 %collective-permute-start.3 = (f32[576,512]{1,0:T(8,128)}, f32[576,512]{1,0:T(8,128)S(1)}, u32[]{:S(2)}, u32[]{:S(2)}) collective-permute-start(f32[576,512]{1,0:T(8,128)} %get-tuple-element.9), channel_id=1, source_target_pairs={{0,8},{8,0},{16,24},{24,16},{1,9},{9,1},{17,25},{25,17},{2,10},{10... | collective-permute-start | bytes 3538952 | tf_op jit(solution)/shard_map/ppermute | solution.py:143
  153.3 51.1 %collective-permute-start.5 = (f32[576,512]{1,0:T(8,128)}, f32[576,512]{1,0:T(8,128)S(1)}, u32[]{:S(2)}, u32[]{:S(2)}) collective-permute-start(f32[576,512]{1,0:T(8,128)} %get-tuple-element.10), channel_id=1, source_target_pairs={{0,24},{8,16},{16,8},{24,0},{1,25},{9,17},{17,9},{25,1},{2,26},{10... | collective-permute-start | bytes 3538952 | tf_op jit(solution)/shard_map/ppermute | solution.py:143
  156.2 49.7 %collective-permute-start.4 = (f32[576,512]{1,0:T(8,128)}, f32[576,512]{1,0:T(8,128)}, u32[]{:S(2)}, u32[]{:S(2)}) collective-permute-start(f32[576,512]{1,0:T(8,128)} %get-tuple-element.11), channel_id=1, source_target_pairs={{0,16},{8,24},{16,0},{24,8},{1,17},{9,25},{17,1},{25,9},{2,18},{10... | collective-permute-start | bytes 3538952 | tf_op jit(solution)/shard_map/ppermute | solution.py:143
  202.9 5.6 %copy-start.1 = (f32[512,512]{1,0:T(8,128)S(1)}, f32[512,512]{1,0:T(8,128)}, u32[]{:S(2)}) copy-start(f32[512,512]{1,0:T(8,128)} %up_ref.1) | copy-start | bytes 3145732
  204.4 1.0 copy-start.3
  208.5 2.1 copy-start
Sparse Core Ops, SparseCore 0:
  9.7 93.4 all-gather.1
  106.6 99.9 reduce-scatter.1
